TPU v7x, 32 devices: a whole 2x2x4 slice. The times are simulated.
32 devices in a mesh: groups: 2 (over y), tile: 4 (over z), row: 2 (over x), lev: 2 (over core).
Axes of the slice: x: 2, y: 2, z: 4, core: 2. Of those that a mesh axis runs over, the one named last changes fastest.
Arguments:
- air_exchange_rates: float32 [8, 1024, 128], P('lev', ('groups', 'tile', 'row')), parts along dimension 1, may hold values from -48 to 48
- outgoing_stripes: int32 [16, 8, 4], P(('groups', 'tile', 'row')), parts along dimension 0, may hold values from 0 to 63
- outgoing_tally: int32 [16, 8], P(('groups', 'tile', 'row')), parts along dimension 0, may hold values from 1 to 4, as said below
- regrid_inputs: int32 [2048, 2, 4], P(('groups', 'tile'), 'row'), parts along dimension 0, may hold values from 0 to 31, as said below
- regrid_factor_id: int32 [2048, 2, 4], P(('groups', 'tile'), 'row'), parts along dimension 0, may hold values from 0 to 15
- regrid_tally: int32 [2048, 2], P(('groups', 'tile'), 'row'), parts along dimension 0, may hold values from 1 to 4, as said below
- intersection_areas: float32 [32, 128, 128], P('groups'), parts along dimension 0, may hold values from 0.002 to 0.014
- sea_indicator: int32 [2048, 256], P(('groups', 'tile'), 'row'), parts along dimension 0, may hold values 0 or 1
- mixing_rate: float32 [2048, 256], P(('groups', 'tile'), 'row'), parts along dimension 0, may hold values from 0.03 to 0.24
- warmth_profile: float32 [16, 2048, 256], P('lev', ('groups', 'tile'), 'row'), parts along dimension 1, may hold values from 0 to 4
- warming_factor: float32 [8, 16], P(None, 'lev'), may hold values from -6 to 6
- stratum_depths: float32 [16], replicated, may hold values from 1 to 10
Outputs:
- warmth_following: float32 [16, 2048, 256], P('lev', ('groups', 'tile'), 'row'), parts along dimension 1
- air_side_skin_heat: float32 [1024, 128], P(('groups', 'tile', 'row')), parts along dimension 0
There are 2 independent parts, one for each index of `groups`. A program takes and returns all parts, laid end to end along the dimension named above; an argument that names none is the same for every part. Nothing has to cross between parts.
Inputs may be any that keep to these rules, and one draw needn't show every extreme that they name: `outgoing_tally`: some ocean tile receives 4 live slots from every owner. `regrid_inputs`: the first listed block (k = 0) of every grid line names a live slot. `regrid_tally`: the first grid line of each tile lists 4 blocks.
All inputs are finite; a program needn't handle non-finite values. No bound on the sum of `sea_indicator` on one device may be relied on, other than what follows from the above.
Results may differ from a plain program's by a relative error of at most 0.0003.
Values sent between devices are 32-bit elements; how exact they have to be, the bound alone decides.
A program may use at most 64 MiB of HBM per device.

v0:
```python
import functools
import jax
import jax.numpy as jnp
from jax import lax
from jax.experimental import pallas as pl
from jax.experimental.pallas import tpu as pltpu
from jax.sharding import PartitionSpec as P

precise = lax.Precision.HIGHEST
f32 = jnp.float32
bf16 = jnp.bfloat16
MESH = pl.DeviceIdType.MESH
SMALL = 16


def halves(v):
    hi = v.astype(bf16)
    return hi, (v - hi.astype(f32)).astype(bf16)


def iota(shape, dim):
    return lax.broadcasted_iota(jnp.int32, shape, dim)


def dot(a, b):
    return jnp.dot(a, b, preferred_element_type=f32)


def window(
    tiles, rows, levs,
    air_ref, stripes_ref, tally_ref, src_ref, wid_ref, cnt_ref, area_ref, sea_ref, mix_ref,
    warm_ref, factor_ref, thick_ref,
    out_ref, skin_ref,
    outbox, inbox, edge, zin, colbuf, xin, dbuf, sel, sel_t, area_t, area_cat, table, base,
    spread, reply, replies,
    flux_send, flux_recv, halo_send, halo_recv, back_send, back_recv,
):
    tile, row, lev = lax.axis_index("tile"), lax.axis_index("row"), lax.axis_index("lev")
    peers = tiles * rows
    count = peers * levs
    me = (tile * rows + row) * levs + lev
    fields, owned, width = air_ref.shape
    slots = stripes_ref.shape[0]
    depth, lines = warm_ref.shape[:2]
    tables = area_ref.shape[0]
    picks = fields * slots
    places = peers * slots

    def device(o):
        return {"tile": o // (rows * levs), "row": (o // levs) % rows, "lev": o % levs}

    barrier = pltpu.get_barrier_semaphore()
    for j in range(1, count):
        pl.semaphore_signal(barrier, inc=1, device_id=device((me + j) % count), device_id_type=MESH)

    live = iota((slots, peers), 0) < tally_ref[...]
    listed = jnp.where(live, stripes_ref[...], -1)
    lane = iota((slots, peers * picks), 1)
    wide = jnp.zeros(lane.shape, jnp.int32)
    for d in range(peers):
        wide = jnp.where(lane // picks == d, listed[:, d : d + 1], wide)
    picked = jnp.sum(
        jnp.where(lane % slots == iota(lane.shape, 0), wide, 0), axis=0, keepdims=True
    )
    total = peers * picks
    at = iota((fields * owned, total), 0)
    to = iota((fields * owned, total), 1)
    chooser = jnp.where(
        jnp.logical_and(at // owned == (to // slots) % fields, at % owned == picked), 1.0, 0.0
    )
    chooser = chooser.T.astype(bf16)
    air_hi, air_lo = halves(air_ref[...].reshape(fields * owned, width))
    outbox[...] = (dot(chooser, air_hi) + dot(chooser, air_lo)).reshape(outbox.shape)

    sea = sea_ref[...].astype(f32)
    mix = mix_ref[...]
    edge[...] = jnp.zeros_like(edge)
    for side, line in ((0, 0), (1, lines - 1)):
        for l in range(depth):
            edge[side, l : l + 1, :] = warm_ref[l, line : line + 1, :]
        edge[side, depth : depth + 1, :] = sea[line : line + 1]
        edge[side, depth + 1 : depth + 2, :] = mix[line : line + 1]
    lane = iota((lines, width), 1)
    packed = jnp.zeros((lines, width), f32)
    for l in range(depth):
        packed = jnp.where(lane == l, warm_ref[l, :, 0:1], packed)
        packed = jnp.where(lane == depth + l, warm_ref[l, :, width - 1 : width], packed)
    packed = jnp.where(lane == 2 * depth, sea[:, 0:1], packed)
    packed = jnp.where(lane == 2 * depth + 1, sea[:, width - 1 : width], packed)
    packed = jnp.where(lane == 2 * depth + 2, mix[:, 0:1], packed)
    packed = jnp.where(lane == 2 * depth + 3, mix[:, width - 1 : width], packed)
    colbuf[...] = packed.T[: 3 * depth]

    pl.semaphore_wait(barrier, count - 1)

    def flux(j):
        o = (me + j) % count
        return pltpu.make_async_remote_copy(
            src_ref=outbox.at[o // levs],
            dst_ref=inbox.at[me],
            send_sem=flux_send.at[j],
            recv_sem=flux_recv.at[j],
            device_id=device(o),
            device_id_type=MESH,
        )

    for j in range(1, count):
        flux(j).start()
    inbox[pl.ds(me, 1)] = outbox[pl.ds(me // levs, 1)]

    halos = (
        (0, tile > 0, tile < tiles - 1, edge.at[0], zin.at[1], {"tile": jnp.maximum(tile - 1, 0)}),
        (1, tile < tiles - 1, tile > 0, edge.at[1], zin.at[0], {"tile": jnp.minimum(tile + 1, tiles - 1)}),
        (2, row > 0, row < rows - 1, colbuf, xin.at[1], {"row": jnp.maximum(row - 1, 0)}),
        (3, row < rows - 1, row > 0, colbuf, xin.at[0], {"row": jnp.minimum(row + 1, rows - 1)}),
    )

    def halo(i):
        n, there, comes, src, dst, target = halos[i]
        return pltpu.make_async_remote_copy(
            src_ref=src,
            dst_ref=dst,
            send_sem=halo_send.at[n],
            recv_sem=halo_recv.at[n],
            device_id=target,
            device_id_type=MESH,
        )

    for i in range(4):
        pl.when(halos[i][1])(lambda i=i: halo(i).start())

        @pl.when(jnp.logical_not(halos[i][2]))
        def _(i=i):
            halos[i][4][...] = jnp.zeros(halos[i][4].shape, f32)

    entry = iota((tables * places, lines), 0)
    counts = jnp.zeros((tables * places, lines), f32)
    for k in range(src_ref.shape[0]):
        ident = jnp.where(
            k < cnt_ref[...], wid_ref[k : k + 1, :] * places + src_ref[k : k + 1, :], -1
        )
        counts = counts + jnp.where(entry == ident, 1.0, 0.0)
    sel_t[...] = counts.astype(bf16)
    counts = counts.T.astype(bf16)
    sel[:, : tables * places] = counts
    sel[:, tables * places :] = counts

    for w in range(tables):
        hi, lo = halves(area_ref[w])
        area_cat[w * width : (w + 1) * width, :width] = hi
        area_cat[w * width : (w + 1) * width, width:] = lo
        hi, lo = halves(area_ref[w].T)
        area_t[0:width, w * width : (w + 1) * width] = hi
        area_t[width : 2 * width, w * width : (w + 1) * width] = lo

    ones = jnp.ones((places, 2 * width), bf16)
    sums = dot(ones, area_t[: 2 * width, :])
    for w in range(tables):
        hi, lo = halves(sums[:, w * width : (w + 1) * width])
        table[w * places : (w + 1) * places, :width] = hi
        table[(tables + w) * places : (tables + w + 1) * places, :width] = lo
    heat_scale = sea / dot(sel[...], table[:, :width])

    def backward(values):
        for w in range(tables):
            hi, lo = halves(values[w * places : (w + 1) * places])
            spread[:places, w * width : (w + 1) * width] = hi
            spread[places:, w * width : (w + 1) * width] = lo
        r = dot(spread[...], area_cat[...])
        return (r[:places, :width] + r[:places, width:]) + (r[places:, :width] + r[places:, width:])

    den = backward(dot(sel_t[...], sea.astype(bf16))) * (1.0 / levs)
    for p in range(peers):
        reply[p, slots : 2 * slots, :] = den[p * slots : (p + 1) * slots]

    size = peers * levs * picks
    by_level = jnp.where(iota((depth * places, depth), 0) // places == iota((depth * places, depth), 1), 1.0, 0.0)
    by_field = jnp.where(
        (iota((levs * fields, size), 1) // slots) % (levs * fields) == iota((levs * fields, size), 0), 1.0, 0.0
    )
    mixer = lax.dot_general(
        by_level, factor_ref[...], (((1,), (1,)), ((), ())), precision=precise, preferred_element_type=f32
    )
    mixer = jnp.dot(mixer, by_field, precision=precise, preferred_element_type=f32)
    r = iota((depth * places, size), 0)
    c = iota((depth * places, size), 1)
    same = jnp.logical_and((r // slots) % peers == c // (levs * picks), r % slots == c % slots)
    mix_hi, mix_lo = halves(jnp.where(same, mixer, 0.0))

    right = 0.5 * (mix + pltpu.roll(mix, width - 1, 1)) * sea * pltpu.roll(sea, width - 1, 1)
    right = jnp.where(lane == width - 1, 0.0, right)
    line = iota((lines, width), 0)
    down = 0.5 * (mix + pltpu.roll(mix, lines - 1, 0)) * sea * pltpu.roll(sea, lines - 1, 0)
    down = jnp.where(line == lines - 1, 0.0, down)
    for i in range(4):
        pl.when(halos[i][2])(lambda i=i: halo(i).wait_recv())
    side = []
    for n, edge_line in ((0, 0), (1, lines - 1)):
        coef = (
            edge[n, depth : depth + 1, :] * zin[n, depth : depth + 1, :] * 0.5
            * (edge[n, depth + 1 : depth + 2, :] + zin[n, depth + 1 : depth + 2, :])
        )
        side.append(coef * (zin[n, :depth, :] - edge[n, :depth, :]))
    dbuf[...] = jnp.zeros_like(dbuf)
    for n in range(2):
        o = 1 - n
        coef = (
            colbuf[2 * depth + n : 2 * depth + n + 1, :]
            * xin[n, 2 * depth + o : 2 * depth + o + 1, :]
            * 0.5
            * (
                colbuf[2 * depth + 2 + n : 2 * depth + 3 + n, :]
                + xin[n, 2 * depth + 2 + o : 2 * depth + 3 + o, :]
            )
        )
        dbuf[n * depth : (n + 1) * depth, :] = coef * (
            xin[n, o * depth : (o + 1) * depth, :] - colbuf[n * depth : (n + 1) * depth, :]
        )
    columns = dbuf[...].T
    for l in range(depth):
        heat = warm_ref[l]
        east = right * (pltpu.roll(heat, width - 1, 1) - heat)
        south = down * (pltpu.roll(heat, lines - 1, 0) - heat)
        moved = heat + ((east - pltpu.roll(east, 1, 1)) + (south - pltpu.roll(south, 1, 0)))
        moved = moved + jnp.where(lane == 0, columns[:, l : l + 1], 0.0)
        moved = moved + jnp.where(lane == width - 1, columns[:, depth + l : depth + l + 1], 0.0)
        moved = moved + jnp.where(line == 0, side[0][l : l + 1], 0.0)
        base[l] = moved + jnp.where(line == lines - 1, side[1][l : l + 1], 0.0)

    for j in range(1, count):
        flux(j).wait_recv()
    got_hi, got_lo = halves(inbox[...].reshape(size, width))
    level_flux = dot(mix_hi, got_hi) + (dot(mix_hi, got_lo) + dot(mix_lo, got_hi))
    g_hi, g_lo = halves(level_flux)
    for w in range(0, tables, 2):
        at = slice(w * width, (w + 2) * width)
        part = dot(g_hi, area_t[:width, at]) + (
            dot(g_hi, area_t[width : 2 * width, at]) + dot(g_lo, area_t[:width, at])
        )
        hi, lo = halves(part)
        for n in range(2):
            for l in range(depth):
                put = slice((w + n) * places, (w + n + 1) * places)
                put_lo = slice((tables + w + n) * places, (tables + w + n + 1) * places)
                rows_l = slice(l * places, (l + 1) * places)
                cols_l = slice(n * width, (n + 1) * width)
                table[put, l * width : (l + 1) * width] = hi[rows_l, cols_l]
                table[put_lo, l * width : (l + 1) * width] = lo[rows_l, cols_l]
    thick_sum = thick_ref[0]
    for l in range(1, levs * depth):
        thick_sum = thick_sum + thick_ref[l]
    surface = jnp.zeros((lines, width), f32)
    for l in range(0, depth, 2):
        heating = dot(sel[...], table[:, l * width : (l + 2) * width])
        for n in range(2):
            heat = base[l + n] + heat_scale * heating[:, n * width : (n + 1) * width]
            out_ref[l + n] = heat
            surface = surface + thick_ref[lev * depth + l + n] * heat
    surface = sea * surface / thick_sum

    hi, lo = halves(surface)
    num = backward(dot(sel_t[...], hi) + dot(sel_t[...], lo))
    for p in range(peers):
        reply[p, :slots, :] = num[p * slots : (p + 1) * slots]

    def back(j):
        o = (me + j) % count
        return pltpu.make_async_remote_copy(
            src_ref=reply.at[o // levs],
            dst_ref=replies.at[me],
            send_sem=back_send.at[j],
            recv_sem=back_recv.at[j],
            device_id=device(o),
            device_id_type=MESH,
        )

    for j in range(1, count):
        back(j).start()
    replies[pl.ds(me, 1)] = reply[pl.ds(me // levs, 1)]
    at = iota((2 * owned, total), 0)
    to = iota((2 * owned, total), 1)
    gather = jnp.where(
        jnp.logical_and(at % owned == picked, at // owned == (to % (2 * slots)) // slots), 1.0, 0.0
    ).astype(bf16)
    for j in range(1, count):
        back(j).wait_recv()
    hi, lo = halves(replies[...].reshape(total, width))
    sums = dot(gather, hi) + dot(gather, lo)
    skin_ref[...] = sums[:owned] / jnp.maximum(sums[owned:], 1.0)

    for j in range(1, count):
        flux(j).wait_send()
        back(j).wait_send()
    for i in range(4):
        pl.when(halos[i][1])(lambda i=i: halo(i).wait_send())


def fused(
    tiles, rows, levs,
    air_exchange_rates, outgoing_stripes, outgoing_tally, regrid_inputs, regrid_factor_id,
    regrid_tally, intersection_areas, sea_indicator, mixing_rate, warmth_profile,
    warming_factor, stratum_depths,
):
    fields, owned, width = air_exchange_rates.shape
    slots = outgoing_stripes.shape[2]
    depth, lines = warmth_profile.shape[:2]
    tables = intersection_areas.shape[0]
    peers = tiles * rows
    count = peers * levs
    places = peers * slots
    vmem = pl.BlockSpec(memory_space=pltpu.VMEM)
    smem = pl.BlockSpec(memory_space=pltpu.SMEM)
    dma = pltpu.SemaphoreType.DMA
    return pl.pallas_call(
        functools.partial(window, tiles, rows, levs),
        out_shape=(
            jax.ShapeDtypeStruct(warmth_profile.shape, f32),
            jax.ShapeDtypeStruct((owned, width), f32),
        ),
        in_specs=[vmem] * 11 + [smem],
        out_specs=(vmem, vmem),
        scratch_shapes=[
            pltpu.VMEM((peers, fields * slots, width), f32),
            pltpu.VMEM((count, fields * slots, width), f32),
            pltpu.VMEM((2, 2 * depth, width), f32),
            pltpu.VMEM((2, 2 * depth, width), f32),
            pltpu.VMEM((3 * depth, lines), f32),
            pltpu.VMEM((2, 3 * depth, lines), f32),
            pltpu.VMEM((width, lines), f32),
            pltpu.VMEM((lines, 2 * tables * places), bf16),
            pltpu.VMEM((tables * places, lines), bf16),
            pltpu.VMEM((2 * width, tables * width), bf16),
            pltpu.VMEM((tables * width, 2 * width), bf16),
            pltpu.VMEM((2 * tables * places, depth * width), bf16),
            pltpu.VMEM((depth, lines, width), f32),
            pltpu.VMEM((2 * places, tables * width), bf16),
            pltpu.VMEM((peers, 2 * slots, width), f32),
            pltpu.VMEM((count, 2 * slots, width), f32),
            dma((count,)), dma((count,)), dma((4,)), dma((4,)), dma((count,)), dma((count,)),
        ],
        compiler_params=pltpu.CompilerParams(
            collective_id=0, has_side_effects=True, vmem_limit_bytes=48 * 1024 * 1024
        ),
        name="window",
    )(
        air_exchange_rates,
        outgoing_stripes[0].T,
        outgoing_tally,
        regrid_inputs[:, 0, :].T,
        regrid_factor_id[:, 0, :].T,
        regrid_tally.T,
        intersection_areas,
        sea_indicator,
        mixing_rate,
        warmth_profile,
        warming_factor,
        stratum_depths,
    )


def extended(cells, sides, width):
    for axis, dim in sides:
        count = lax.axis_size(axis)
        ends = count - 1
        head = lax.slice_in_dim(cells, 0, width, axis=dim)
        tail = lax.slice_in_dim(cells, cells.shape[dim] - width, cells.shape[dim], axis=dim)
        cells = jnp.concatenate(
            [
                lax.ppermute(tail, axis, [(i, (i + 1) % count) for i in range(ends)]),
                cells,
                lax.ppermute(head, axis, [((i + 1) % count, i) for i in range(ends)]),
            ],
            axis=dim,
        )
    return cells


def shards(
    air_exchange_rates,
    outgoing_stripes,
    outgoing_tally,
    regrid_inputs,
    regrid_factor_id,
    regrid_tally,
    intersection_areas,
    sea_indicator,
    mixing_rate,
    warmth_profile,
    warming_factor,
    stratum_depths,
):
    tile_count = lax.axis_size("tile")
    row_count = lax.axis_size("row")
    peer_count = tile_count * row_count
    field_count, atm_rows, width = air_exchange_rates.shape
    slot_count = outgoing_stripes.shape[2]
    marine_stripes = warmth_profile.shape[1]
    depth_tally = warmth_profile.shape[0]
    block_most = regrid_inputs.shape[2]
    table_size = intersection_areas.shape[0]
    row_list = outgoing_stripes[0].reshape(-1)
    live_slot = (
        (jnp.arange(slot_count, dtype=jnp.int32)[None, :] < outgoing_tally[0][:, None])
        .reshape(-1)
        .astype(jnp.float32)
    )
    picker = (row_list[:, None] == jnp.arange(atm_rows, dtype=jnp.int32)[None, :]).astype(
        jnp.float32
    ) * live_slot[:, None]
    outgoing = jnp.einsum("qa,fac->qfc", picker, air_exchange_rates, precision=precise)
    arrived = lax.all_to_all(outgoing, ("tile", "row"), split_axis=0, concat_axis=0, tiled=True)
    source_slot = regrid_inputs[:, 0, :]
    weight_id = regrid_factor_id[:, 0, :]
    block_count = regrid_tally[:, 0]
    usable = (jnp.arange(block_most, dtype=jnp.int32)[None, :] < block_count[:, None]).astype(
        jnp.float32
    )
    selector = (
        weight_id[:, :, None] == jnp.arange(table_size, dtype=jnp.int32)[None, None, :]
    ).astype(jnp.float32) * usable[:, :, None]
    fetched = arrived[source_slot]
    grouped = jnp.einsum("xkw,xkfc->wxfc", selector, fetched, precision=precise)
    summed = jnp.einsum("wec,wxfc->fxe", intersection_areas, grouped, precision=precise)
    coverage = jnp.einsum(
        "xkw,we->xe", selector, jnp.sum(intersection_areas, axis=2), precision=precise
    )
    local_flux = summed / coverage[None]
    all_flux = lax.all_gather(local_flux, "lev", axis=0, tiled=True)
    thermal_tendency = jnp.einsum("fl,fxc->lxc", warming_factor, all_flux, precision=precise)
    marine_indicator = sea_indicator.astype(jnp.float32)
    piled_arrays = jnp.concatenate(
        [warmth_profile, marine_indicator[None], mixing_rate[None]], axis=0
    )
    padded = extended(piled_arrays, (("tile", 1), ("row", 2)), 1)
    spread_tracer = jnp.zeros_like(warmth_profile)
    for step_x, step_y in ((1, 0), (-1, 0), (0, 1), (0, -1)):
        neighbour_values = padded[
            :, 1 + step_x : 1 + step_x + marine_stripes, 1 + step_y : 1 + step_y + width
        ]
        spread_tracer = spread_tracer + neighbour_values[depth_tally] * 0.5 * (
            mixing_rate + neighbour_values[depth_tally + 1]
        ) * (neighbour_values[:depth_tally] - warmth_profile)
    warmth_following = warmth_profile + marine_indicator * (spread_tracer + thermal_tendency)
    level_start = lax.axis_index("lev") * depth_tally
    own_thick = lax.dynamic_slice_in_dim(stratum_depths, level_start, depth_tally)
    partial_value = jnp.einsum(
        "l,lxc->xc", own_thick, warmth_following, precision=precise
    ) / jnp.sum(stratum_depths)
    topmost_stratum = lax.psum(partial_value, "lev")
    columns = intersection_areas.shape[2]
    coupled_entries = jnp.stack([marine_indicator * topmost_stratum, marine_indicator], axis=1)
    spread = jnp.einsum("wec,xje->wxjc", intersection_areas, coupled_entries, precision=precise)
    contribution = jnp.einsum("xkw,wxjc->xkjc", selector, spread, precision=precise)
    target = (
        source_slot.reshape(-1)[:, None]
        == jnp.arange(peer_count * slot_count, dtype=jnp.int32)[None, :]
    ).astype(jnp.float32)
    returning = jnp.einsum(
        "rq,rjc->qjc",
        target,
        contribution.reshape(marine_stripes * block_most, 2, columns),
        precision=precise,
    )
    returned = lax.all_to_all(
        returning.reshape(peer_count, slot_count, 2, columns),
        ("tile", "row"),
        split_axis=0,
        concat_axis=0,
        tiled=True,
    )
    returned = returned.reshape(peer_count * slot_count, 2, columns)
    atm_sums = jnp.einsum("qa,qjc->ajc", picker, returned, precision=precise)
    dividend_sum = atm_sums[:, 0]
    divisor_sum = atm_sums[:, 1]
    air_side_skin_heat = dividend_sum / jnp.maximum(divisor_sum, 1.0)
    return (warmth_following, air_side_skin_heat)


def solution(mesh):
    placed = (
        P("lev", ("groups", "tile", "row"), None),
        P(("groups", "tile", "row"), None, None),
        P(("groups", "tile", "row"), None),
        P(("groups", "tile"), "row", None),
        P(("groups", "tile"), "row", None),
        P(("groups", "tile"), "row"),
        P("groups", None, None),
        P(("groups", "tile"), "row"),
        P(("groups", "tile"), "row"),
        P("lev", ("groups", "tile"), "row"),
        P(None, "lev"),
        P(),
    )
    tiles, rows, levs = mesh.shape["tile"], mesh.shape["row"], mesh.shape["lev"]
    small = tiles * rows * levs <= SMALL and levs == 2
    return jax.shard_map(
        functools.partial(fused, tiles, rows, levs) if small else shards,
        mesh=mesh,
        in_specs=placed,
        out_specs=(P("lev", ("groups", "tile"), "row"), P(("groups", "tile", "row"), None)),
        check_vma=False,
    )
```

profile of v0, /device:TPU:0, one launch (start us, length us, event | category | flops | bytes accessed | tf_op | source)
XLA Modules:
  0.0 29.8 jit_solution(10687802487907537039)
XLA Ops:
  0.6 0.0 copy-start.5
  0.6 0.0 copy-start.8
  0.7 0.0 copy-start.9
  0.7 0.0 copy-start.10
  0.7 0.6 %copy-done.5 = s32[256,1,4]{0,2,1:T(4,128)S(1)} copy-done((s32[256,1,4]{0,2,1:T(4,128)S(1)}, s32[256,1,4]{0,2,1:T(4,128)}, u32[]{:S(2)}) %copy-start.5) | copy-done | bytes 4120
  1.3 0.0 copy-done.8
  1.3 0.0 copy-done.9
  1.3 0.0 copy-done.10
  1.3 0.0 copy-start
  1.4 1.2 %copy-done = f32[16,128,128]{2,1,0:T(8,128)S(1)} copy-done((f32[16,128,128]{2,1,0:T(8,128)S(1)}, f32[16,128,128]{2,1,0:T(8,128)}, u32[]{:S(2)}) %copy-start) | copy-done | bytes 1048600
  2.6 0.0 copy-start.1
  2.6 1.2 %copy-done.1 = f32[8,256,128]{2,1,0:T(8,128)S(1)} copy-done((f32[8,256,128]{2,1,0:T(8,128)S(1)}, f32[8,256,128]{2,1,0:T(8,128)}, u32[]{:S(2)}) %copy-start.1) | copy-done | bytes 1048600
  3.8 0.0 copy-start.2
  3.8 0.9 %copy-done.2 = f32[4,64,128]{2,1,0:T(8,128)S(1)} copy-done((f32[4,64,128]{2,1,0:T(8,128)S(1)}, f32[4,64,128]{2,1,0:T(8,128)}, u32[]{:S(2)}) %copy-start.2) | copy-done | bytes 131096
  4.7 0.0 copy-start.3
  4.7 0.9 %copy-done.3 = s32[256,128]{1,0:T(8,128)S(1)} copy-done((s32[256,128]{1,0:T(8,128)S(1)}, s32[256,128]{1,0:T(8,128)}, u32[]{:S(2)}) %copy-start.3) | copy-done | bytes 131096
  5.6 0.0 copy-start.4
  5.6 0.9 %copy-done.4 = f32[256,128]{1,0:T(8,128)S(1)} copy-done((f32[256,128]{1,0:T(8,128)S(1)}, f32[256,128]{1,0:T(8,128)}, u32[]{:S(2)}) %copy-start.4) | copy-done | bytes 131096
  6.5 0.0 copy-start.6
  6.5 0.7 %copy-done.6 = s32[256,1,4]{0,2,1:T(4,128)S(1)} copy-done((s32[256,1,4]{0,2,1:T(4,128)S(1)}, s32[256,1,4]{0,2,1:T(4,128)}, u32[]{:S(2)}) %copy-start.6) | copy-done | bytes 4120
  7.2 0.0 copy-start.7
  7.2 0.7 %copy-done.7 = f32[8,8]{1,0:T(8,128)S(1)} copy-done((f32[8,8]{1,0:T(8,128)S(1)}, f32[8,8]{1,0:T(8,128)}, u32[]{:S(2)}) %copy-start.7) | copy-done | bytes 280
  7.9 0.0 copy-start.11
  7.9 0.7 %copy-done.11 = f32[16]{0:T(128)S(1)} copy-done((f32[16]{0:T(128)S(1)}, f32[16]{0:T(128)}, u32[]{:S(2)}) %copy-start.11) | copy-done | bytes 88
  8.5 19.6 %window.1 = (f32[8,256,128]{2,1,0:T(8,128)S(1)}, f32[64,128]{1,0:T(8,128)S(1)}) custom-call(f32[4,64,128]{2,1,0:T(8,128)S(1)} %copy-done.2, s32[4,8]{1,0:T(4,128)S(1)} %bitcast.12, s32[1,8]{1,0:T(1,128)S(1)} %copy-done.10, s32[4,256]{1,0:T(4,128)S(1)} %bitcast.10, s32[4,256]{1,0:T(4,128)S(1)} %bitcast.11, s32[1,256]{1,0:T(1,128)S(1)} %bitcast.13, ...), custom_call_target="tpu_custom_call" | custom-call | tf_op jit(solution)/shard_map/window/pallas_call | solution.py:314
  28.2 1.0 %copy.16 = f32[8,256,128]{2,1,0:T(8,128)} copy(f32[8,256,128]{2,1,0:T(8,128)S(1)} %get-tuple-element.4) | data formatting | bytes 2097152
  29.2 0.6 %copy.17 = f32[64,128]{1,0:T(8,128)} copy(f32[64,128]{1,0:T(8,128)S(1)} %get-tuple-element.5) | data formatting | bytes 65536
Async XLA Ops:
  0.6 0.7 %copy-start.5 = (s32[256,1,4]{0,2,1:T(4,128)S(1)}, s32[256,1,4]{0,2,1:T(4,128)}, u32[]{:S(2)}) copy-start(s32[256,1,4]{0,2,1:T(4,128)} %param.15) | copy-start | bytes 12292
  0.6 0.7 %copy-start.8 = (s32[1,8,4]{1,2,0:T(4,128)S(1)}, s32[1,8,4]{1,2,0:T(4,128)}, u32[]{:S(2)}) copy-start(s32[1,8,4]{1,2,0:T(4,128)} %param.13) | copy-start | bytes 388
  0.7 0.7 %copy-start.9 = (s32[256,1]{0,1:T(1,128)S(1)}, s32[256,1]{0,1:T(1,128)}, u32[]{:S(2)}) copy-start(s32[256,1]{0,1:T(1,128)} %param.17) | copy-start | bytes 3076
  0.7 0.7 %copy-start.10 = (s32[1,8]{1,0:T(1,128)S(1)}, s32[1,8]{1,0:T(1,128)}, u32[]{:S(2)}) copy-start(s32[1,8]{1,0:T(1,128)} %tally_ref.1) | copy-start | bytes 100
  1.3 1.2 %copy-start = (f32[16,128,128]{2,1,0:T(8,128)S(1)}, f32[16,128,128]{2,1,0:T(8,128)}, u32[]{:S(2)}) copy-start(f32[16,128,128]{2,1,0:T(8,128)} %area_ref.1) | copy-start | bytes 3145732
  2.6 1.2 %copy-start.1 = (f32[8,256,128]{2,1,0:T(8,128)S(1)}, f32[8,256,128]{2,1,0:T(8,128)}, u32[]{:S(2)}) copy-start(f32[8,256,128]{2,1,0:T(8,128)} %warm_ref.1) | copy-start | bytes 3145732
  3.8 0.9 %copy-start.2 = (f32[4,64,128]{2,1,0:T(8,128)S(1)}, f32[4,64,128]{2,1,0:T(8,128)}, u32[]{:S(2)}) copy-start(f32[4,64,128]{2,1,0:T(8,128)} %air_ref.1) | copy-start | bytes 393220
  4.7 0.9 %copy-start.3 = (s32[256,128]{1,0:T(8,128)S(1)}, s32[256,128]{1,0:T(8,128)}, u32[]{:S(2)}) copy-start(s32[256,128]{1,0:T(8,128)} %sea_ref.1) | copy-start | bytes 393220
  5.6 0.9 %copy-start.4 = (f32[256,128]{1,0:T(8,128)S(1)}, f32[256,128]{1,0:T(8,128)}, u32[]{:S(2)}) copy-start(f32[256,128]{1,0:T(8,128)} %mix_ref.1) | copy-start | bytes 393220
  6.5 0.7 %copy-start.6 = (s32[256,1,4]{0,2,1:T(4,128)S(1)}, s32[256,1,4]{0,2,1:T(4,128)}, u32[]{:S(2)}) copy-start(s32[256,1,4]{0,2,1:T(4,128)} %param.16) | copy-start | bytes 12292
  7.2 0.7 %copy-start.7 = (f32[8,8]{1,0:T(8,128)S(1)}, f32[8,8]{1,0:T(8,128)}, u32[]{:S(2)}) copy-start(f32[8,8]{1,0:T(8,128)} %factor_ref.1) | copy-start | bytes 772
  7.9 0.7 %copy-start.11 = (f32[16]{0:T(128)S(1)}, f32[16]{0:T(128)}, u32[]{:S(2)}) copy-start(f32[16]{0:T(128)} %thick_ref.1) | copy-start | bytes 196
where the time goes:
time: 30.1 us; the launch traced here: 29.8 us
  Pallas kernels  19.6 us (65%)
  local copies, waits for them, and re-layouts  9.46 us (31%)
  between operations  0.69 us (2%)
    pallas_call x1, Pallas kernels, fused(): pl.pallas_call(functools.partial(window, tiles, rows, levs), out_shape=(j...  19.6 us
    unnamed x26, local copies, waits for them, and re-layouts  9.46 us

commit v1 on v0

--- a/solution.py
+++ b/solution.py
@@ -10,6 +10,7 @@
 f32 = jnp.float32
 bf16 = jnp.bfloat16
 MESH = pl.DeviceIdType.MESH
+FIRST, SECOND, THIRD = (1, 2, 0), (7, 8, 9), (3, 4, 5, 6, 10, 11)
 SMALL = 16
 
 
@@ -28,6 +29,20 @@
 
 def window(
     tiles, rows, levs,
+    *refs,
+):
+    sources, (out_ref, skin_ref), held = refs[:12], refs[12:14], refs[14:26]
+    loads = [
+        pltpu.make_async_copy(source, target, refs[-1].at[n])
+        for n, (source, target) in enumerate(zip(sources, held))
+    ]
+    for n in FIRST + SECOND + THIRD:
+        loads[n].start()
+    exchange(tiles, rows, levs, loads, *held, out_ref, skin_ref, *refs[26:-1])
+
+
+def exchange(
+    tiles, rows, levs, loads,
     air_ref, stripes_ref, tally_ref, src_ref, wid_ref, cnt_ref, area_ref, sea_ref, mix_ref,
     warm_ref, factor_ref, thick_ref,
     out_ref, skin_ref,
@@ -53,6 +68,9 @@
     for j in range(1, count):
         pl.semaphore_signal(barrier, inc=1, device_id=device((me + j) % count), device_id_type=MESH)
 
+    for n in FIRST:
+        loads[n].wait()
+
     live = iota((slots, peers), 0) < tally_ref[...]
     listed = jnp.where(live, stripes_ref[...], -1)
     lane = iota((slots, peers * picks), 1)
@@ -72,6 +90,8 @@
     air_hi, air_lo = halves(air_ref[...].reshape(fields * owned, width))
     outbox[...] = (dot(chooser, air_hi) + dot(chooser, air_lo)).reshape(outbox.shape)
 
+    for n in SECOND:
+        loads[n].wait()
     sea = sea_ref[...].astype(f32)
     mix = mix_ref[...]
     edge[...] = jnp.zeros_like(edge)
@@ -132,6 +152,9 @@
         @pl.when(jnp.logical_not(halos[i][2]))
         def _(i=i):
             halos[i][4][...] = jnp.zeros(halos[i][4].shape, f32)
+
+    for n in THIRD:
+        loads[n].wait()
 
     entry = iota((tables * places, lines), 0)
     counts = jnp.zeros((tables * places, lines), f32)
@@ -309,7 +332,20 @@
     count = peers * levs
     places = peers * slots
     vmem = pl.BlockSpec(memory_space=pltpu.VMEM)
-    smem = pl.BlockSpec(memory_space=pltpu.SMEM)
+    operands = (
+        air_exchange_rates,
+        outgoing_stripes[0].T,
+        outgoing_tally,
+        regrid_inputs[:, 0, :].T,
+        regrid_factor_id[:, 0, :].T,
+        regrid_tally.T,
+        intersection_areas,
+        sea_indicator,
+        mixing_rate,
+        warmth_profile,
+        warming_factor,
+        stratum_depths,
+    )
     dma = pltpu.SemaphoreType.DMA
     return pl.pallas_call(
         functools.partial(window, tiles, rows, levs),
@@ -317,9 +353,11 @@
             jax.ShapeDtypeStruct(warmth_profile.shape, f32),
             jax.ShapeDtypeStruct((owned, width), f32),
         ),
-        in_specs=[vmem] * 11 + [smem],
+        in_specs=[pl.BlockSpec(memory_space=pltpu.HBM)] * 12,
         out_specs=(vmem, vmem),
-        scratch_shapes=[
+        scratch_shapes=[pltpu.VMEM(x.shape, x.dtype) for x in operands[:11]]
+        + [pltpu.SMEM(stratum_depths.shape, f32)]
+        + [
             pltpu.VMEM((peers, fields * slots, width), f32),
             pltpu.VMEM((count, fields * slots, width), f32),
             pltpu.VMEM((2, 2 * depth, width), f32),
@@ -337,25 +375,13 @@
             pltpu.VMEM((peers, 2 * slots, width), f32),
             pltpu.VMEM((count, 2 * slots, width), f32),
             dma((count,)), dma((count,)), dma((4,)), dma((4,)), dma((count,)), dma((count,)),
+            dma((12,)),
         ],
         compiler_params=pltpu.CompilerParams(
-            collective_id=0, has_side_effects=True, vmem_limit_bytes=48 * 1024 * 1024
+            collective_id=0, has_side_effects=True, vmem_limit_bytes=60 * 1024 * 1024
         ),
         name="window",
-    )(
-        air_exchange_rates,
-        outgoing_stripes[0].T,
-        outgoing_tally,
-        regrid_inputs[:, 0, :].T,
-        regrid_factor_id[:, 0, :].T,
-        regrid_tally.T,
-        intersection_areas,
-        sea_indicator,
-        mixing_rate,
-        warmth_profile,
-        warming_factor,
-        stratum_depths,
-    )
+    )(*operands)
 
 
 def extended(cells, sides, width):

time: 30.1 us -> 23.9 us (0.79)
  local copies, waits for them, and re-layouts: 9.46 us -> 2.89 us
  Pallas kernels: 19.6 us -> 20.2 us
    unnamed x26 -> x4, local copies, waits for them, and re-layouts: 9.46 us -> 2.89 us
    pallas_call x1, Pallas kernels: 19.6 us -> 20.2 us  [fused(): pl.pallas_call(functools.partial(window, tiles, rows, levs), out_shape=(j...]
where the time goes in v1:
time: 23.9 us; the launch traced here: 23.8 us
  Pallas kernels  20.2 us (85%)
  local copies, waits for them, and re-layouts  2.89 us (12%)
  between operations  0.65 us (3%)
    pallas_call x1, Pallas kernels, fused(): pl.pallas_call(functools.partial(window, tiles, rows, levs), out_shape=(j...  20.2 us
    unnamed x4, local copies, waits for them, and re-layouts  2.89 us

profile of v1, /device:TPU:0, one launch (start us, length us, event | category | flops | bytes accessed | tf_op | source)
XLA Modules:
  0.0 23.8 jit_solution(14898582099235810151)
XLA Ops:
  0.6 20.2 %window.1 = (f32[8,256,128]{2,1,0:T(8,128)}, f32[64,128]{1,0:T(8,128)}) custom-call(f32[4,64,128]{2,1,0:T(8,128)} %refs_0_.1, s32[4,8]{1,0:T(4,128)} %bitcast.12, s32[1,8]{1,0:T(1,128)} %refs_2_.1, s32[4,256]{1,0:T(4,128)} %bitcast.10, s32[4,256]{1,0:T(4,128)} %bitcast.11, s32[1,256]{1,0:T(1,128)} %bitcast.13, f32[16,128,128]{2,1,0:T(8,128)} %refs_6_.1, ...), custom_call_target="tpu_custom_call" | custom-call | tf_op jit(solution)/shard_map/window/pallas_call | solution.py:350
  20.9 0.0 copy-start
  20.9 2.3 %copy.16 = f32[8,256,128]{2,1,0:T(8,128)} copy(f32[8,256,128]{2,1,0:T(8,128)} %get-tuple-element.4) | data formatting | bytes 2097152
  23.1 0.0 copy-done
  23.1 0.6 %copy.17 = f32[64,128]{1,0:T(8,128)} copy(f32[64,128]{1,0:T(8,128)S(1)} %copy-done) | data formatting | bytes 65536
Async XLA Ops:
  20.9 2.3 %copy-start = (f32[64,128]{1,0:T(8,128)S(1)}, f32[64,128]{1,0:T(8,128)}, u32[]{:S(2)}) copy-start(f32[64,128]{1,0:T(8,128)} %get-tuple-element.5) | copy-start | bytes 98308

commit v2 on v1

--- a/solution.py
+++ b/solution.py
@@ -350,8 +350,8 @@
     return pl.pallas_call(
         functools.partial(window, tiles, rows, levs),
         out_shape=(
-            jax.ShapeDtypeStruct(warmth_profile.shape, f32),
-            jax.ShapeDtypeStruct((owned, width), f32),
+            pltpu.VMEM(warmth_profile.shape, f32),
+            pltpu.VMEM((owned, width), f32),
         ),
         in_specs=[pl.BlockSpec(memory_space=pltpu.HBM)] * 12,
         out_specs=(vmem, vmem),

time: 23.9 us -> 21.6 us (0.904)
  local copies, waits for them, and re-layouts: 2.89 us -> 1.59 us
  Pallas kernels: 20.2 us -> 19.2 us
    unnamed x4 -> x2, local copies, waits for them, and re-layouts: 2.89 us -> 1.59 us
    pallas_call x1, Pallas kernels: 20.2 us -> 19.2 us  [fused(): pl.pallas_call(functools.partial(window, tiles, rows, levs), out_shape=(p...]
where the time goes in v2:
time: 21.6 us; the launch traced here: 21.5 us
  Pallas kernels  19.2 us (89%)
  local copies, waits for them, and re-layouts  1.59 us (7%)
  between operations  0.64 us (3%)
    pallas_call x1, Pallas kernels, fused(): pl.pallas_call(functools.partial(window, tiles, rows, levs), out_shape=(p...  19.2 us
    unnamed x2, local copies, waits for them, and re-layouts  1.59 us

profile of v2, /device:TPU:0, one launch (start us, length us, event | category | flops | bytes accessed | tf_op | source)
XLA Modules:
  0.0 21.5 jit_solution(13747926459218925038)
XLA Ops:
  0.6 19.2 %window.1 = (f32[8,256,128]{2,1,0:T(8,128)S(1)}, f32[64,128]{1,0:T(8,128)S(1)}) custom-call(f32[4,64,128]{2,1,0:T(8,128)} %refs_0_.1, s32[4,8]{1,0:T(4,128)} %bitcast.12, s32[1,8]{1,0:T(1,128)} %refs_2_.1, s32[4,256]{1,0:T(4,128)} %bitcast.10, s32[4,256]{1,0:T(4,128)} %bitcast.11, s32[1,256]{1,0:T(1,128)} %bitcast.13, f32[16,128,128]{2,1,0:T(8,128)} %refs_6_.1, ...), custom_call_target="tpu_custom_call" | custom-call | tf_op jit(solution)/shard_map/window/pallas_call | solution.py:350
  19.9 1.0 %copy.16 = f32[8,256,128]{2,1,0:T(8,128)} copy(f32[8,256,128]{2,1,0:T(8,128)S(1)} %get-tuple-element.2) | data formatting | bytes 2097152
  20.8 0.6 %copy.17 = f32[64,128]{1,0:T(8,128)} copy(f32[64,128]{1,0:T(8,128)S(1)} %get-tuple-element.3) | data formatting | bytes 65536
